TPU v7x, 32 devices: a whole 2x2x4 slice. The times are simulated.
32 devices in a mesh: groups: 2 (over y), rows: 4 (over z), reps: 2 (over x), cols: 2 (over core).
Axes of the slice: x: 2, y: 2, z: 4, core: 2. Of those that a mesh axis runs over, the one named last changes fastest.
Arguments:
- scalars: bfloat16 [256, 4096], P(None, ('groups', 'rows', 'reps', 'cols')), parts along dimension 1, may hold values from -6 to 6
- vectors: bfloat16 [3, 64, 4096], P(None, None, ('groups', 'rows', 'reps', 'cols')), parts along dimension 2, may hold values from -6 to 6
- positions: bfloat16 [3, 4096], P(None, ('groups', 'rows', 'reps', 'cols')), parts along dimension 1, may hold values from -5 to 5
- node_pose: int32 [4096], P(('groups', 'rows', 'reps', 'cols')), parts along dimension 0, may hold values from 0 to 3, never falling along the last dimension, each value on 1 to 768 neighbouring positions
- source_block: int32 [512], P(('groups', 'rows', 'reps', 'cols')), parts along dimension 0, may hold values from 0 to 15, as said below
- target_block: int32 [512], P(('groups', 'rows', 'reps', 'cols')), parts along dimension 0, may hold values from 0 to 15, as said below
- block_count: int32 [32], P(('groups', 'rows', 'reps', 'cols')), parts along dimension 0, may hold values from 11 to 16, as said below
- shell_codes: int32 [512, 128, 128], P(('groups', 'rows', 'reps', 'cols')), parts along dimension 0, may hold values from 0 to 10
- weight_in: bfloat16 [256, 256], replicated, may hold values from -0.375 to 0.375
- message_weight: bfloat16 [384, 256], replicated, may hold values from -0.375 to 0.375
- filter_weights: bfloat16 [10, 384], replicated, may hold values from -0.125 to 0.125
- read_scalar: float32 [256], replicated, may hold values from -4 to 4
- read_vector: float32 [64], replicated, may hold values from -0.12 to 0.12
- targets: float32 [8], P('groups'), parts along dimension 0, may hold values from -6 to 6
Outputs:
- new_scalars: bfloat16 [256, 4096], P(None, ('groups', 'rows', 'reps', 'cols')), parts along dimension 1
- new_vectors: bfloat16 [3, 64, 4096], P(None, None, ('groups', 'rows', 'reps', 'cols')), parts along dimension 2
- scores: float32 [8], P('groups'), parts along dimension 0
- forces: float32 [3, 4096], P(None, ('groups', 'rows', 'reps', 'cols')), parts along dimension 1
There are 2 independent parts, one for each index of `groups`. A program takes and returns all parts, laid end to end along the dimension named above; an argument that names none is the same for every part. Nothing has to cross between parts.
Inputs may be any that keep to these rules, and one draw needn't show every extreme that they name: With g = e // 16: source_block[e] // 4 equals g // 4, and source_block[e] % 2 equals g % 2. With g = e // 16: (target_block[e] // 2) % 2 equals (g // 2) % 2. Two slots of one group whose offsets within the group differ by less than 8 name different target blocks. block_count[g] counts the live slots g * 16 to g * 16 + block_count[g] - 1; some group has all 16 live. node_pose never falls along the atoms; every pose has 1 to 768 atoms, one exactly 768.
All inputs are finite; a program needn't handle non-finite values.
Results may differ from a plain program's by a relative error of at most 0.017.
Values may be sent and summed in bfloat16 or wider, within the bound.
A program may use at most 128 MiB of HBM per device.

v0:
```python
import jax
import jax.numpy as jnp
from jax import lax
from jax.sharding import PartitionSpec as P

POSE_ATOMS = 512


def filtered(gates, vectors, positions, filter_weights, scalar_width, vector_width):
    weights_t = filter_weights.astype(jnp.float32).T
    gates = gates.astype(jnp.float32)
    vectors = vectors.astype(jnp.float32)
    positions = positions.astype(jnp.float32)
    scalar_part = gates[..., :scalar_width, None, :] * weights_t[:scalar_width, :, None]
    gate_vec = gates[..., scalar_width : scalar_width + vector_width, :]
    gate_pos = gates[..., scalar_width + vector_width :, :]
    vector_part = (
        gate_vec[..., None, :, None, :]
        * vectors[..., :, :, None, :]
        * weights_t[scalar_width : scalar_width + vector_width, :, None]
    )
    vector_part = (
        vector_part
        + gate_pos[..., None, :, None, :]
        * positions[..., :, None, None, :]
        * weights_t[scalar_width + vector_width :, :, None]
    )
    norm_part = gate_pos[..., :, None, :] * weights_t[scalar_width + vector_width :, :, None]
    leading = gates.shape[:-2]
    columns = weights_t.shape[1] * gates.shape[-1]
    stacked = jnp.concatenate(
        [
            scalar_part.reshape(leading + (scalar_width, columns)),
            vector_part.reshape(leading + (3 * vector_width, columns)),
            norm_part.reshape(leading + (vector_width, columns)),
        ],
        axis=-2,
    )
    return stacked.astype(jnp.bfloat16)


def message_inputs(scalars, weight_in, message_weight):
    hidden = jax.nn.silu(
        jnp.einsum("oi,...ib->...ob", weight_in, scalars, preferred_element_type=jnp.float32)
    ).astype(jnp.bfloat16)
    return jnp.einsum(
        "oi,...ib->...ob", message_weight, hidden, preferred_element_type=jnp.float32
    ).astype(jnp.bfloat16)


def local(
    scalars,
    vectors,
    positions,
    node_pose,
    source_block,
    target_block,
    block_count,
    shell_codes,
    weight_in,
    message_weight,
    filter_weights,
    read_scalar,
    read_vector,
    targets,
):
    row_count = lax.axis_size("rows")
    rep_count = lax.axis_size("reps")
    col_count = lax.axis_size("cols")
    scalar_width = scalars.shape[0]
    vector_width = vectors.shape[1]
    block_width = scalars.shape[1]
    shell_count = filter_weights.shape[0]
    slot_total = shell_codes.shape[0]
    place_count = row_count * col_count
    panel_scalars, panel_vectors, panel_positions = (
        lax.all_gather(scalars[None], "reps", axis=0, tiled=True),
        lax.all_gather(vectors[None], "reps", axis=0, tiled=True),
        lax.all_gather(positions[None], "reps", axis=0, tiled=True),
    )
    panel_gates = message_inputs(panel_scalars, weight_in, message_weight)
    own_gates = lax.dynamic_index_in_dim(panel_gates, lax.axis_index("reps"), 0, keepdims=False)
    panel_rows = filtered(
        panel_gates, panel_vectors, panel_positions, filter_weights, scalar_width, vector_width
    )
    out_rows = panel_rows.shape[1]
    source_local = source_block // col_count % rep_count
    target_local = target_block // (rep_count * col_count) * col_count + target_block % col_count
    offsets = jnp.arange(slot_total, dtype=jnp.int32)
    live = (offsets < block_count[0]).astype(jnp.bfloat16)
    levels = jnp.arange(1, shell_count + 1, dtype=jnp.int32)
    tables = (shell_codes[:, None, :, :] == levels[None, :, None, None]).astype(
        jnp.bfloat16
    ) * live[:, None, None, None]
    target_onehot = (
        target_local[:, None] == jnp.arange(place_count, dtype=jnp.int32)[None, :]
    ).astype(jnp.float32)
    source_onehot = (
        source_local[:, None] == jnp.arange(rep_count, dtype=jnp.int32)[None, :]
    ).astype(jnp.float32)
    group_size = 4
    block_total = slot_total // group_size
    table_blocks = tables.reshape(block_total, group_size, shell_count, block_width, block_width)
    source_blocks = source_local.reshape(block_total, group_size)
    target_blocks = target_local.reshape(block_total, group_size)
    target_hot_blocks = target_onehot.reshape(block_total, group_size, place_count)
    source_hot_blocks = source_onehot.reshape(block_total, group_size, rep_count)

    def forward_step(totals, inputs):
        table_part, source_part, place_hot = inputs
        left = jnp.take(panel_rows, source_part, axis=0)
        term = jnp.einsum(
            "eck,ekb->ecb",
            left,
            table_part.reshape(group_size, shell_count * block_width, block_width),
            preferred_element_type=jnp.float32,
        )
        placed = jnp.einsum("ep,ecb->pcb", place_hot, term, precision=lax.Precision.HIGHEST)
        return (totals + placed, None)

    totals, _ = lax.scan(
        forward_step,
        jnp.zeros((place_count, out_rows, block_width), jnp.float32),
        (table_blocks, source_blocks, target_hot_blocks),
    )
    partial_value = totals.astype(jnp.bfloat16)
    received = lax.all_to_all(
        partial_value, ("rows", "cols"), split_axis=0, concat_axis=0, tiled=True
    )
    message = jnp.sum(received, axis=0, dtype=jnp.float32)
    delta_vec = message[scalar_width : scalar_width + 3 * vector_width].reshape(
        3, vector_width, block_width
    )
    norm_term = message[scalar_width + 3 * vector_width :]
    new_scalars = (scalars.astype(jnp.float32) + message[:scalar_width]).astype(jnp.bfloat16)
    new_vectors = (
        vectors.astype(jnp.float32)
        + delta_vec
        - positions.astype(jnp.float32)[:, None, :] * norm_term[None]
    ).astype(jnp.bfloat16)
    scalar_float = new_scalars.astype(jnp.float32)
    vector_float = new_vectors.astype(jnp.float32)
    energy = jnp.sum(read_scalar[:, None] * scalar_float, axis=0) + jnp.sum(
        read_vector[:, None] * jnp.sum(vector_float * vector_float, axis=0), axis=0
    )
    pose_count = targets.shape[0]
    member = (node_pose[None, :] == jnp.arange(pose_count, dtype=jnp.int32)[:, None]).astype(
        jnp.float32
    )
    scores = lax.psum(jnp.sum(member * energy[None], axis=1), ("rows", "reps", "cols")) / POSE_ATOMS
    node_resid = jnp.sum(member * (scores - targets)[:, None], axis=0)
    grad_vec = (2.0 * node_resid[None, None, :] * read_vector[None, :, None] * vector_float).astype(
        jnp.bfloat16
    )
    grad_all = lax.all_gather(
        grad_vec.reshape(1, 3 * vector_width, block_width), ("rows", "cols"), axis=0, tiled=True
    )
    weight_rows = jnp.tile(
        filter_weights[:, scalar_width + vector_width :].astype(jnp.float32), (1, 3)
    ).T

    def backward_step(back_totals, inputs):
        table_part, target_part, source_hot = inputs
        right = jnp.take(grad_all, target_part, axis=0)
        product = jnp.einsum(
            "eri,ekji->erkj", right, table_part, preferred_element_type=jnp.float32
        )
        term = jnp.sum(product * weight_rows[None, :, :, None], axis=2)
        placed = jnp.einsum("en,erj->nrj", source_hot, term, precision=lax.Precision.HIGHEST)
        return (back_totals + placed, None)

    back_panel, _ = lax.scan(
        backward_step,
        jnp.zeros((rep_count, 3 * vector_width, block_width), jnp.float32),
        (table_blocks, target_blocks, source_hot_blocks),
    )
    back_own = (
        lax.psum_scatter(back_panel.astype(jnp.bfloat16), "reps", scatter_dimension=0, tiled=True)
        .astype(jnp.float32)[0]
        .reshape(3, vector_width, block_width)
    )
    gate_pos = own_gates[scalar_width + vector_width :].astype(jnp.float32)
    forces = jnp.sum(norm_term[None] * grad_vec.astype(jnp.float32), axis=1) - jnp.sum(
        gate_pos[None] * back_own, axis=1
    )
    return (new_scalars, new_vectors, scores, forces)


def solution(mesh):
    placed = (
        P(None, ("groups", "rows", "reps", "cols")),
        P(None, None, ("groups", "rows", "reps", "cols")),
        P(None, ("groups", "rows", "reps", "cols")),
        P(("groups", "rows", "reps", "cols")),
        P(("groups", "rows", "reps", "cols")),
        P(("groups", "rows", "reps", "cols")),
        P(("groups", "rows", "reps", "cols")),
        P(("groups", "rows", "reps", "cols"), None, None),
        P(),
        P(),
        P(),
        P(),
        P(),
        P("groups"),
    )
    return jax.shard_map(
        local,
        mesh=mesh,
        in_specs=placed,
        out_specs=(
            P(None, ("groups", "rows", "reps", "cols")),
            P(None, None, ("groups", "rows", "reps", "cols")),
            P("groups"),
            P(None, ("groups", "rows", "reps", "cols")),
        ),
        check_vma=False,
    )
```

profile of v0, /device:TPU:0, one launch (start us, length us, event | category | flops | bytes accessed | tf_op | source)
XLA Modules:
  0.0 234.7 jit_solution(17919921275558122679)
XLA Ops:
  7.2 6.2 %all-gather = bf16[512,128]{1,0:T(8,128)(2,1)S(1)} all-gather(bf16[256,128]{1,0:T(8,128)(2,1)} %param.18), channel_id=2, replica_groups=mesh['groups'=2,'rows'=4,'reps'=2,'cols'=2] {'reps'}, dimensions={0}, use_global_device_ids=true | all-gather | bytes 196608 | tf_op jit(solution)/shard_map/all_gather | solution.py:77
  16.9 4.2 %all-gather.3 = bf16[2,3,128]{2,1,0:T(4,128)(2,1)S(1)} all-gather(bf16[1,3,128]{2,1,0:T(4,128)(2,1)S(1)} %bitcast.127), channel_id=4, replica_groups=mesh['groups'=2,'rows'=4,'reps'=2,'cols'=2] {'reps'}, dimensions={0}, use_global_device_ids=true | all-gather | bytes 2304 | tf_op jit(solution)/shard_map/all_gather | solution.py:79
  22.9 3.2 %copy.91 = f32[2,192,1280]{1,2,0:T(8,128)} copy(f32[2,192,1280]{2,1,0:T(8,128)} %mul.256) | data formatting | bytes 3932160 | tf_op jit(solution)/shard_map/mul | solution.py:24
  26.1 4.8 %all-gather.1 = bf16[6,64,128]{2,1,0:T(8,128)(2,1)S(1)} all-gather(bf16[3,64,128]{2,1,0:T(8,128)(2,1)S(1)} %copy-done.9), channel_id=3, replica_groups=mesh['groups'=2,'rows'=4,'reps'=2,'cols'=2] {'reps'}, dimensions={0}, use_global_device_ids=true | all-gather | bytes 147456 | tf_op jit(solution)/shard_map/all_gather | solution.py:78
  36.3 2.7 %copy.90 = f32[192,1280]{0,1:T(8,128)} copy(f32[192,1280]{1,0:T(8,128)} %bitcast.117) | data formatting | bytes 1966080 | tf_op jit(solution)/shard_map/mul | solution.py:24
  40.6 2.7 %copy.86 = f32[192,1280]{0,1:T(8,128)} copy(f32[192,1280]{1,0:T(8,128)} %bitcast.118) | data formatting | bytes 1966080 | tf_op jit(solution)/shard_map/mul | solution.py:18
  48.7 3.0 %copy.96 = bf16[2,512,1280]{2,1,0:T(8,128)(2,1)S(1)} copy(bf16[2,512,1280]{1,2,0:T(8,128)(2,1)} %pad_maximum_fusion) | data formatting | bytes 5242880
  52.6 4.8 %compare_select_fusion.4 = bf16[4,4,10,128,128]{4,3,2,1,0:T(8,128)(2,1)} fusion(s32[4,4,128,128]{3,2,1,0:T(8,128)} %bitcast.120, s32[10]{0:T(128)S(1)} %copy-done.18, bf16[4,4]{1,0:T(4,128)(2,1)S(1)} %fusion.37), kind=kLoop, calls=%fused_computation.40 | loop fusion | flops 5242880 | bytes 6291528 | tf_op jit(solution)/shard_map/mul | solution.py:92
  57.4 61.2 %while.22 = (s32[]{:T(128)}, f32[8,512,128]{2,0,1:T(8,128)}, f32[4,4,8]{2,1,0:T(4,128)S(1)}, s32[4,4]{1,0:T(4,128)S(1)}, bf16[2,512,1280]{2,1,0:T(8,128)(2,1)S(1...) while((s32[]{:T(128)}, f32[8,512,128]{2,0,1:T(8,128)}, ...), condition=%wide.region_1.2_spmd.clone, body=%wide.region_0.1_spmd.clone.sunk | while | flops 699925568 | bytes 25958596 | solution.py:121
  57.4 3.2 %gather_fusion = bf16[4,512,1280]{2,1,0:T(8,128)(2,1)} fusion(bf16[2,512,1280]{2,1,0:T(8,128)(2,1)S(1)} %get-tuple-element.285, s32[1024]{0:T(1024)S(1)} %pad_clamp_fusion.4), kind=kCustom, calls=%fused_computation.clone.clone.1 | custom fusion | bytes 10485776 | tf_op jit(solution)/shard_map/while/body/eval_jaxpr/jit(_take)/gather | solution.py:111
  62.1 5.1 %fusion.64 = f32[4,512,128]{2,1,0:T(8,128)} fusion(bf16[4,1280,128]{2,1,0:T(8,128)(2,1)S(1)} %bitcast.113, bf16[4,512,1280]{2,1,0:T(8,128)(2,1)} %gather_fusion, pred[4]{0:T(512)(128)(4,1)S(1)} %compare_and_fusion.4), kind=kOutput, calls=%fused_computation.3.clone.1 | convolution fusion | flops 673710080 | bytes 7602180 | tf_op jit(solution)/shard_map/while/body/eval_jaxpr/eck,ekb->ecb/dot_general | solution.py:112
  67.2 5.2 %select_add_fusion.2 = f32[8,512,128]{2,0,1:T(8,128)} fusion(f32[8,512,128]{2,0,1:T(8,128)} %get-tuple-element.274, f32[4,512,128]{2,1,0:T(8,128)} %fusion.64, pred[]{:T(512)S(6)} %compare.12, f32[4,4,8]{2,1,0:T(4,128)S(1)} %get-tuple-element.283, s32[]{:T(128)} %get-tuple-element.273), kind=kOutput, calls=%fused_computation.7.clone.1 | convolution fusion | flops 26214400 | bytes 5244933 | tf_op jit(solution)/shard_map/while/body/eval_jaxpr/ep,ecb->pcb/dot_general | solution.py:118
  72.5 3.2 %gather_fusion = bf16[4,512,1280]{2,1,0:T(8,128)(2,1)} fusion(bf16[2,512,1280]{2,1,0:T(8,128)(2,1)S(1)} %get-tuple-element.285, s32[1024]{0:T(1024)S(1)} %pad_clamp_fusion.4), kind=kCustom, calls=%fused_computation.clone.clone.1 | custom fusion | bytes 10485776 | tf_op jit(solution)/shard_map/while/body/eval_jaxpr/jit(_take)/gather | solution.py:111
  77.2 5.1 %fusion.64 = f32[4,512,128]{2,1,0:T(8,128)} fusion(bf16[4,1280,128]{2,1,0:T(8,128)(2,1)S(1)} %bitcast.113, bf16[4,512,1280]{2,1,0:T(8,128)(2,1)} %gather_fusion, pred[4]{0:T(512)(128)(4,1)S(1)} %compare_and_fusion.4), kind=kOutput, calls=%fused_computation.3.clone.1 | convolution fusion | flops 673710080 | bytes 7602180 | tf_op jit(solution)/shard_map/while/body/eval_jaxpr/eck,ekb->ecb/dot_general | solution.py:112
  82.3 5.6 %select_add_fusion.2 = f32[8,512,128]{2,0,1:T(8,128)} fusion(f32[8,512,128]{2,0,1:T(8,128)} %get-tuple-element.274, f32[4,512,128]{2,1,0:T(8,128)} %fusion.64, pred[]{:T(512)S(6)} %compare.12, f32[4,4,8]{2,1,0:T(4,128)S(1)} %get-tuple-element.283, s32[]{:T(128)} %get-tuple-element.273), kind=kOutput, calls=%fused_computation.7.clone.1 | convolution fusion | flops 26214400 | bytes 5244933 | tf_op jit(solution)/shard_map/while/body/eval_jaxpr/ep,ecb->pcb/dot_general | solution.py:118
  87.9 3.2 %gather_fusion = bf16[4,512,1280]{2,1,0:T(8,128)(2,1)} fusion(bf16[2,512,1280]{2,1,0:T(8,128)(2,1)S(1)} %get-tuple-element.285, s32[1024]{0:T(1024)S(1)} %pad_clamp_fusion.4), kind=kCustom, calls=%fused_computation.clone.clone.1 | custom fusion | bytes 10485776 | tf_op jit(solution)/shard_map/while/body/eval_jaxpr/jit(_take)/gather | solution.py:111
  92.6 5.1 %fusion.64 = f32[4,512,128]{2,1,0:T(8,128)} fusion(bf16[4,1280,128]{2,1,0:T(8,128)(2,1)S(1)} %bitcast.113, bf16[4,512,1280]{2,1,0:T(8,128)(2,1)} %gather_fusion, pred[4]{0:T(512)(128)(4,1)S(1)} %compare_and_fusion.4), kind=kOutput, calls=%fused_computation.3.clone.1 | convolution fusion | flops 673710080 | bytes 7602180 | tf_op jit(solution)/shard_map/while/body/eval_jaxpr/eck,ekb->ecb/dot_general | solution.py:112
  97.7 5.6 %select_add_fusion.2 = f32[8,512,128]{2,0,1:T(8,128)} fusion(f32[8,512,128]{2,0,1:T(8,128)} %get-tuple-element.274, f32[4,512,128]{2,1,0:T(8,128)} %fusion.64, pred[]{:T(512)S(6)} %compare.12, f32[4,4,8]{2,1,0:T(4,128)S(1)} %get-tuple-element.283, s32[]{:T(128)} %get-tuple-element.273), kind=kOutput, calls=%fused_computation.7.clone.1 | convolution fusion | flops 26214400 | bytes 5244933 | tf_op jit(solution)/shard_map/while/body/eval_jaxpr/ep,ecb->pcb/dot_general | solution.py:118
  103.3 3.2 %gather_fusion = bf16[4,512,1280]{2,1,0:T(8,128)(2,1)} fusion(bf16[2,512,1280]{2,1,0:T(8,128)(2,1)S(1)} %get-tuple-element.285, s32[1024]{0:T(1024)S(1)} %pad_clamp_fusion.4), kind=kCustom, calls=%fused_computation.clone.clone.1 | custom fusion | bytes 10485776 | tf_op jit(solution)/shard_map/while/body/eval_jaxpr/jit(_take)/gather | solution.py:111
  108.0 5.1 %fusion.64 = f32[4,512,128]{2,1,0:T(8,128)} fusion(bf16[4,1280,128]{2,1,0:T(8,128)(2,1)S(1)} %bitcast.113, bf16[4,512,1280]{2,1,0:T(8,128)(2,1)} %gather_fusion, pred[4]{0:T(512)(128)(4,1)S(1)} %compare_and_fusion.4), kind=kOutput, calls=%fused_computation.3.clone.1 | convolution fusion | flops 673710080 | bytes 7602180 | tf_op jit(solution)/shard_map/while/body/eval_jaxpr/eck,ekb->ecb/dot_general | solution.py:112
  113.0 5.6 %select_add_fusion.2 = f32[8,512,128]{2,0,1:T(8,128)} fusion(f32[8,512,128]{2,0,1:T(8,128)} %get-tuple-element.274, f32[4,512,128]{2,1,0:T(8,128)} %fusion.64, pred[]{:T(512)S(6)} %compare.12, f32[4,4,8]{2,1,0:T(4,128)S(1)} %get-tuple-element.283, s32[]{:T(128)} %get-tuple-element.273), kind=kOutput, calls=%fused_computation.7.clone.1 | convolution fusion | flops 26214400 | bytes 5244933 | tf_op jit(solution)/shard_map/while/body/eval_jaxpr/ep,ecb->pcb/dot_general | solution.py:118
  118.6 3.0 %copy.116 = bf16[8,512,128]{2,1,0:T(8,128)(2,1)} copy(f32[8,512,128]{2,0,1:T(8,128)} %get-tuple-element.73) | data formatting | bytes 3145728 | tf_op jit(solution)/shard_map/while | solution.py:121
  121.7 5.5 %all-to-all-start = ((bf16[8,512,128]{2,1,0:T(8,128)(2,1)}), bf16[8,512,128]{2,1,0:T(8,128)(2,1)S(1)}, u32[]{:S(2)}, u32[]{:S(2)}) async-start(bf16[8,512,128]{2,1,0:T(8,128)(2,1)} %copy.116), calls=%async_computation | async-start | bytes 2097152 | tf_op jit(solution)/shard_map/all_to_all | solution.py:127
  128.3 25.5 %all-to-all-done = bf16[8,512,128]{2,1,0:T(8,128)(2,1)S(1)} async-done(((bf16[8,512,128]{2,1,0:T(8,128)(2,1)}), bf16[8,512,128]{2,1,0:T(8,128)(2,1)S(1)}, u32[]{:S(2)}, u32[]{:S(2)}) %all-to-all-start) | async-done | bytes 1048608 | tf_op jit(solution)/shard_map/all_to_all | solution.py:127
  155.0 31.3 %psum.7 = f32[4]{0:T(128)S(1)} all-reduce(f32[4]{0:T(128)S(1)} %select_reduce_fusion.1), channel_id=1, replica_groups=mesh['groups'=2,'rows'=4,'reps'=2,'cols'=2] {'rows','reps','cols'}, use_global_device_ids=true, to_apply=%region_7.8 | all-reduce | flops 4 | bytes 32 | tf_op jit(solution)/shard_map/psum | solution.py:150
  187.0 14.5 %all_gather.15 = bf16[8,192,128]{2,1,0:T(8,128)(2,1)S(1)} all-gather(bf16[1,192,128]{2,1,0:T(8,128)(2,1)S(1)} %bitcast.124), channel_id=1, replica_groups=mesh['groups'=2,'rows'=4,'reps'=2,'cols'=2] {'rows','cols'}, dimensions={0}, use_global_device_ids=true | all-gather | bytes 442368 | tf_op jit(solution)/shard_map/all_gather | solution.py:155
  201.5 16.8 %while.23 = (s32[]{:T(128)}, f32[2,192,128]{2,0,1:T(2,128)S(1)}, f32[4,4,2]{1,2,0:T(2,128)S(1)}, s32[4,4]{1,0:T(4,128)S(1)}, bf16[8,192,128]{2,1,0:T(8,128)(2,1)...) while((s32[]{:T(128)}, f32[2,192,128]{2,0,1:T(2,128)S(1)}, ...), condition=%wide.region_12.13_spmd.clone, body=%wide.region_10.12_spmd.clone.sunk | while | flops 256082976 | bytes 3119307 | solution.py:172
  202.2 2.1 multiply_reduce_fusion.5
  206.4 2.1 multiply_reduce_fusion.5
  210.6 2.1 multiply_reduce_fusion.5
  214.8 2.1 multiply_reduce_fusion.5
  219.1 7.3 %reduce-scatter.2.cloned.1.call-done = bf16[1,192,128]{2,1,0:T(8,128)(2,1)} async-done(((bf16[2,192,128]{2,1,0:T(8,128)(2,1)}), bf16[1,192,128]{2,1,0:T(8,128)(2,1)}) %reduce-scatter.2.cloned.1.call-update) | async-done | bytes 49168 | tf_op jit(solution)/shard_map/reduce_scatter | solution.py:178
  (154 shorter events, 37.0 us)
Async XLA Ops:
  7.2 6.3 %copy-start = (bf16[384,256]{1,0:T(8,128)(2,1)S(1)}, bf16[384,256]{1,0:T(8,128)(2,1)}, u32[]{:S(2)}) copy-start(bf16[384,256]{1,0:T(8,128)(2,1)} %param.27) | copy-start | bytes 589828
  7.2 8.5 %copy-start.13 = (bf16[10,384]{1,0:T(8,128)(2,1)S(1)}, bf16[10,384]{1,0:T(8,128)(2,1)}, u32[]{:S(2)}) copy-start(bf16[10,384]{1,0:T(8,128)(2,1)} %param.28) | copy-start | bytes 23044
  7.2 9.7 %copy-start.14 = (bf16[3,128]{1,0:T(4,128)(2,1)S(1)}, bf16[3,128]{1,0:T(4,128)(2,1)}, u32[]{:S(2)}) copy-start(bf16[3,128]{1,0:T(4,128)(2,1)} %param.20) | copy-start | bytes 2308
  14.8 6.4 %copy-start.6 = (bf16[2,128,384]{2,1,0:T(8,128)(2,1)}, bf16[2,128,384]{2,1,0:T(8,128)(2,1)S(1)}, u32[]{:S(2)}) copy-start(bf16[2,128,384]{2,1,0:T(8,128)(2,1)S(1)} %convolution_convert_fusion) | copy-start | bytes 589828
  14.8 0.8 copy-start.4
  15.7 7.2 %copy-start.11 = (f32[384,10]{0,1:T(8,128)}, f32[384,10]{0,1:T(8,128)S(1)}, u32[]{:S(2)}) copy-start(f32[384,10]{0,1:T(8,128)S(1)} %convert_bitcast_fusion.1) | copy-start | bytes 46084
  22.9 3.2 %copy-start.5 = (f32[2,64,128]{1,2,0:T(8,128)S(1)}, f32[2,64,128]{1,2,0:T(8,128)}, u32[]{:S(2)}) copy-start(f32[2,64,128]{1,2,0:T(8,128)} %get-tuple-element.181) | copy-start | bytes 196612
  22.9 3.3 %copy-start.9 = (bf16[3,64,128]{2,1,0:T(8,128)(2,1)S(1)}, bf16[3,64,128]{2,1,0:T(8,128)(2,1)}, u32[]{:S(2)}) copy-start(bf16[3,64,128]{2,1,0:T(8,128)(2,1)} %param.19) | copy-start | bytes 147460
  34.9 4.0 %copy-start.12 = (f32[64,10]{0,1:T(8,128)S(1)}, f32[64,10]{0,1:T(8,128)}, u32[]{:S(2)}) copy-start(f32[64,10]{0,1:T(8,128)} %get-tuple-element.183) | copy-start | bytes 7684
  40.6 2.9 %slice-start.1 = ((f32[384,10]{0,1:T(8,128)}), f32[256,10]{0,1:T(8,128)S(1)}, s32[]{:S(2)}) async-start(f32[384,10]{0,1:T(8,128)} %copy-done.11), calls=%async_computation.4 | async-start | bytes 32768 | tf_op jit(solution)/shard_map/slice | solution.py:14
  40.6 3.0 %slice-start = ((f32[2,384,128]{1,2,0:T(8,128)}), f32[2,256,128]{1,2,0:T(8,128)S(1)}, s32[]{:S(2)}) async-start(f32[2,384,128]{1,2,0:T(8,128)} %copy-done.4), calls=%async_computation.3 | async-start | bytes 524288 | tf_op jit(solution)/shard_map/slice | solution.py:14
  43.4 1.7 copy-start.1
  43.4 2.1 copy-start.2
  43.4 2.5 %copy-start.3 = (f32[192,1280]{0,1:T(8,128)S(1)}, f32[192,1280]{0,1:T(8,128)}, u32[]{:S(2)}) copy-start(f32[192,1280]{0,1:T(8,128)} %copy.86) | copy-start | bytes 2949124
  48.6 3.7 %copy-start.20 = (s32[16]{0:T(128)S(1)}, s32[16]{0:T(128)}, u32[]{:S(2)}) copy-start(s32[16]{0:T(128)} %param.23) | copy-start | bytes 196
  48.6 3.9 %copy-start.21 = (s32[16]{0:T(128)S(1)}, s32[16]{0:T(128)}, u32[]{:S(2)}) copy-start(s32[16]{0:T(128)} %param.22) | copy-start | bytes 196
  48.6 4.0 %copy-start.18 = (s32[10]{0:T(128)S(1)}, s32[10]{0:T(128)}, u32[]{:S(2)}) copy-start(s32[10]{0:T(128)} %iota_add_fusion) | copy-start | bytes 124
  118.6 8.8 %copy-start.15 = (bf16[3,128]{1,0:T(4,128)(2,1)S(1)}, bf16[3,128]{1,0:T(4,128)(2,1)}, u32[]{:S(2)}) copy-start(bf16[3,128]{1,0:T(4,128)(2,1)} %param.20) | copy-start | bytes 2308
  118.6 8.8 %copy-start.7 = (bf16[2,128,384]{2,1,0:T(8,128)(2,1)S(1)}, bf16[2,128,384]{2,1,0:T(8,128)(2,1)}, u32[]{:S(2)}) copy-start(bf16[2,128,384]{2,1,0:T(8,128)(2,1)} %copy-done.6) | copy-start | bytes 589828
  121.7 32.3 %copy-start.8 = (bf16[256,128]{1,0:T(8,128)(2,1)S(1)}, bf16[256,128]{1,0:T(8,128)(2,1)}, u32[]{:S(2)}) copy-start(bf16[256,128]{1,0:T(8,128)(2,1)} %param.18) | copy-start | bytes 196612
  121.7 32.3 %copy-start.17 = (f32[256]{0:T(256)S(1)}, f32[256]{0:T(256)}, u32[]{:S(2)}) copy-start(f32[256]{0:T(256)} %param.29) | copy-start | bytes 3076
  121.7 33.0 %copy-start.16 = (f32[64]{0:T(128)S(1)}, f32[64]{0:T(128)}, u32[]{:S(2)}) copy-start(f32[64]{0:T(128)} %param.30) | copy-start | bytes 772
  121.7 33.1 %copy-start.22 = (s32[128]{0:T(128)S(1)}, s32[128]{0:T(128)}, u32[]{:S(2)}) copy-start(s32[128]{0:T(128)} %param.21) | copy-start | bytes 1540
  121.7 64.6 %copy-start.19 = (f32[4]{0:T(128)S(1)}, f32[4]{0:T(128)}, u32[]{:S(2)}) copy-start(f32[4]{0:T(128)} %param.31) | copy-start | bytes 52
  121.7 32.1 %all-to-all-start = ((bf16[8,512,128]{2,1,0:T(8,128)(2,1)}), bf16[8,512,128]{2,1,0:T(8,128)(2,1)S(1)}, u32[]{:S(2)}, u32[]{:S(2)}) async-start(bf16[8,512,128]{2,1,0:T(8,128)(2,1)} %copy.116), calls=%async_computation | async-start | bytes 2097152 | tf_op jit(solution)/shard_map/all_to_all | solution.py:127
  127.2 99.2 %reduce-scatter.2.cloned.1.call-start = ((), (), s32[]{:S(2)}) async-start(), calls=%async_computation.2 | async-start | bytes 147456 | tf_op jit(solution)/shard_map/reduce_scatter | solution.py:178
  154.7 46.8 %copy-start.10 = (bf16[3,64,128]{2,1,0:T(8,128)(2,1)}, bf16[3,64,128]{2,1,0:T(8,128)(2,1)S(1)}, u32[]{:S(2)}) copy-start(bf16[3,64,128]{2,1,0:T(8,128)(2,1)S(1)} %get-tuple-element.178) | copy-start | bytes 147460
Sparse Core Ops, SparseCore 0:
  219.1 7.3 reduce-scatter.1
where the time goes:
time: 236 us; the launch traced here: 235 us
  blocking collectives  61.1 us (26%)
  matrix products  57.4 us (24%)
  local copies, waits for them, and re-layouts  49.3 us (21%)
  waiting for transfers between devices  32.9 us (14%)
  between operations  15.1 us (6%)
  other arithmetic  12.9 us (5%)
  starting transfers between devices  5.73 us (2%)
    psum x1, blocking collectives, local(): lax.psum(jnp.sum(member * energy[None], axis=1), ('rows', 'reps', 'cols'))  31.3 us
    all_to_all x1, waiting for transfers between devices, local(): lax.all_to_all(partial_value, ('rows', 'cols'), split_axis=0, concat_axis...  25.5 us
    dot_general x4, matrix products, forward_step(): jnp.einsum('ep,ecb->pcb', place_hot, term, precision=lax.Precision.HIGHEST)  22 us
    dot_general x4, matrix products, forward_step(): jnp.einsum('eck,ekb->ecb', left, table_part.reshape(group_size, shell_cou...  20.3 us
    all_gather x1, blocking collectives, local(): lax.all_gather(grad_vec.reshape(1, 3 * vector_width, block_width), ('rows...  14.5 us
    gather x4, local copies, waits for them, and re-layouts, forward_step(): left = jnp.take(panel_rows, source_part, axis=0)  12.8 us
    dot_general x4, matrix products, backward_step(): jnp.einsum('eri,ekji->erkj', right, table_part, preferred_element_type=jn...  8.31 us
    unnamed x49, local copies, waits for them, and re-layouts  7.79 us
  transfers between devices with their start and end apart: 2, of which 2 were waited for; matrix products, arithmetic and copies ran while one was open for 0% of the time, Pallas kernels for 0%

commit v1 on v0

v1 whole, which is shorter than its diff:
```python
import functools

import jax
import jax.numpy as jnp
from jax import lax
from jax.experimental import pallas as pl
from jax.experimental.pallas import tpu as pltpu
from jax.sharding import PartitionSpec as P

POSE_ATOMS = 512
BF = jnp.bfloat16
F32 = jnp.float32
MESH = pl.DeviceIdType.MESH
HIGHEST = lax.Precision.HIGHEST


def kernel(
    rows, reps, cols, poses, shells,
    scalars, vectors, positions, node_pose, source_block, target_block, block_count, codes_hbm,
    weight_in, message_weight, filter_weights, read_scalar, read_vector, targets,
    out_scalars, out_vectors, out_scores, out_forces,
    codes, panel_s, panel_v, panel_p, gate_pos, rows_f, fwb, rv_col, xsend, xrecv, own, ssend, recv,
    norm_buf, gather, energies, force_acc, force_recv, force_norm,
    codes_sem, panel_send, panel_recv, x_send, x_recv, s_send, s_recv,
    g_send, g_recv, f_send, e_send, e_recv, q_send, q_recv,
):
    row = lax.axis_index("rows")
    rep = lax.axis_index("reps")
    col = lax.axis_index("cols")
    total = rows * reps * cols
    me = (row * reps + rep) * cols + col
    s_ch = scalars.shape[0]
    v3 = vectors.shape[0]
    v_ch = v3 // 3
    blk = scalars.shape[1]
    slots = codes.shape[0]
    places = rows * cols
    windows = -(-slots // places)
    pose_pad = energies.shape[1]

    def peer(q):
        flat = lax.rem(me + q, total)
        return flat, {
            "rows": flat // (reps * cols),
            "reps": lax.rem(flat // cols, reps),
            "cols": lax.rem(flat, cols),
        }

    barrier = pltpu.get_barrier_semaphore()

    def greet(q, carry):
        pl.semaphore_signal(barrier, inc=1, device_id=peer(q)[1], device_id_type=MESH)
        return carry

    lax.fori_loop(1, total, greet, 0)
    codes_copy = pltpu.make_async_copy(codes_hbm, codes, codes_sem)
    codes_copy.start()

    panel_p[rep] = jnp.zeros((8, blk), F32)
    panel_p[rep, 0:3, :] = positions[...].astype(F32)
    panel_s[rep] = scalars[...]
    panel_v[rep] = vectors[...]
    lane_shell = lax.broadcasted_iota(jnp.int32, (shells, shells * blk), 1) // blk
    sub_shell = lax.broadcasted_iota(jnp.int32, (shells, shells * blk), 0)
    spread = jnp.where(lane_shell == sub_shell, 1.0, 0.0).astype(BF)
    fwb[...] = lax.dot_general(
        filter_weights[...], spread, (((0,), (0,)), ((), ())), preferred_element_type=F32
    )
    rv_row = jnp.concatenate([read_vector[...], jnp.zeros((1, 128 - v_ch), F32)], axis=1)
    rv_col[...] = jnp.transpose(jnp.broadcast_to(rv_row, (blk, 128)))[:v_ch]

    pl.semaphore_wait(barrier, total - 1)

    def panel_copies(q, src_rep):
        out = []
        for a, buf in enumerate((panel_s, panel_v, panel_p)):
            out.append(
                pltpu.make_async_remote_copy(
                    src_ref=buf.at[src_rep],
                    dst_ref=buf.at[src_rep],
                    send_sem=panel_send.at[a, q],
                    recv_sem=panel_recv.at[a, src_rep],
                    device_id={"reps": q},
                    device_id_type=MESH,
                )
            )
        return out

    for o in range(1, reps):
        for c in panel_copies(lax.rem(rep + o, reps), rep):
            c.start()

    def make_rows(q):
        hidden = jnp.dot(weight_in[...], panel_s[q], preferred_element_type=F32)
        hidden = (hidden / (1.0 + jnp.exp(-hidden))).astype(BF)
        gates = jnp.dot(message_weight[...], hidden, preferred_element_type=F32).astype(BF)
        gates = gates.astype(F32)
        gs = gates[:s_ch]
        gv = gates[s_ch : s_ch + v_ch]
        gp = gates[s_ch + v_ch :]
        gate_pos[q] = gp
        pos = panel_p[q]
        vec = panel_v[q].astype(F32)
        gvv = [gv * vec[d * v_ch : (d + 1) * v_ch] for d in range(3)]
        gpp = [gp * pos[d : d + 1] for d in range(3)]
        for k in range(shells):
            span = pl.ds(k * blk, blk)
            rows_f[q, 0:s_ch, span] = (gs * fwb[0:s_ch, span]).astype(BF)
            wv = fwb[s_ch : s_ch + v_ch, span]
            wp = fwb[s_ch + v_ch :, span]
            for d in range(3):
                rows_f[q, s_ch + d * v_ch : s_ch + (d + 1) * v_ch, span] = (
                    gvv[d] * wv + gpp[d] * wp
                ).astype(BF)
            rows_f[q, s_ch + v3 :, span] = (gp * wp).astype(BF)

    def rows_step(o, carry):
        q = lax.rem(rep + o, reps)

        @pl.when(o > 0)
        def _():
            for c in panel_copies(q, q):
                c.wait_recv()

        make_rows(q)
        return carry

    lax.fori_loop(0, reps, rows_step, 0)
    codes_copy.wait()

    def find(r, c, t):
        wanted = (r * reps + rep) * cols + c
        slot = jnp.int32(0)
        found = jnp.int32(0)
        for o in range(t * places, min((t + 1) * places, slots)):
            hit = (target_block[o] == wanted) & (o < block_count[0])
            slot = jnp.where(hit, o, slot)
            found = jnp.where(hit, 1, found)
        src = lax.rem(source_block[slot] // cols, reps)
        return codes[slot] * found, src

    def one_hot(code, axis):
        return jnp.concatenate(
            [jnp.where(code == k + 1, 1.0, 0.0).astype(BF) for k in range(shells)], axis=axis
        )

    def partial(r, c):
        acc = None
        for t in range(windows):
            code, src = find(r, c, t)
            term = jnp.dot(rows_f[src], one_hot(code, 0), preferred_element_type=F32)
            acc = term if acc is None else acc + term
        return acc

    def row_of(s):
        offset = 1 + lax.rem(rows // 2 - 1 + s, rows - 1)
        return lax.rem(row + jnp.where(s == rows - 1, 0, offset), rows)

    def cross(s, o, arriving):
        if arriving:
            mine = o - 1
        else:
            mine = cols - o - 1
        return pltpu.make_async_remote_copy(
            src_ref=xsend.at[s, o - 1],
            dst_ref=xrecv.at[s, mine],
            send_sem=x_send.at[s, o - 1],
            recv_sem=x_recv.at[s, mine],
            device_id={"cols": lax.rem(col + o, cols)},
            device_id_type=MESH,
        )

    def along(s, src_row):
        return pltpu.make_async_remote_copy(
            src_ref=ssend.at[s],
            dst_ref=recv.at[src_row],
            send_sem=s_send.at[s],
            recv_sem=s_recv.at[src_row],
            device_id={"rows": row_of(s)},
            device_id_type=MESH,
        )

    def finish(s):
        for o in range(1, cols):
            cross(s, o, True).wait_recv()
        both = own[s]
        for o in range(1, cols):
            both = both + xrecv[s, o - 1].astype(F32)
        return both

    def forward_step(s, carry):
        r = row_of(s)
        for o in range(1, cols):
            xsend[s, o - 1] = partial(r, lax.rem(col + o, cols)).astype(BF)
            cross(s, o, False).start()

        @pl.when(s > 0)
        def _():
            ssend[s - 1] = finish(s - 1).astype(BF)
            along(s - 1, row).start()

        own[s] = partial(r, col)
        return carry

    lax.fori_loop(0, rows, forward_step, 0)
    last = rows - 1
    own[last] = finish(last)
    for s in range(rows - 1):
        along(s, row_of(s)).wait_recv()

    def message(lo, hi):
        acc = own[last, lo:hi]
        for s in range(rows - 1):
            acc = acc + recv[row_of(s), lo:hi].astype(F32)
        return acc

    norm = message(s_ch + v3, s_ch + v3 + v_ch)
    norm_buf[...] = norm
    pos_own = panel_p[rep]
    square = jnp.zeros((v_ch, blk), F32)
    for d in range(3):
        lo = d * v_ch
        nv = (
            vectors[lo : lo + v_ch].astype(F32)
            + message(s_ch + lo, s_ch + lo + v_ch)
            - pos_own[d : d + 1] * norm
        ).astype(BF)
        out_vectors[lo : lo + v_ch] = nv
        gather[row, col, lo : lo + v_ch] = nv
        nv = nv.astype(F32)
        square = square + nv * nv
    pose_row = node_pose[...]
    gather[row, col, v3 : v3 + 16] = jnp.broadcast_to(pose_row.astype(F32), (16, blk)).astype(BF)

    def spread_row(o, src_row):
        return pltpu.make_async_remote_copy(
            src_ref=gather.at[src_row, col],
            dst_ref=gather.at[src_row, col],
            send_sem=g_send.at[o],
            recv_sem=g_recv.at[src_row, col],
            device_id={"rows": lax.rem(row + o, rows)},
            device_id_type=MESH,
        )

    def spread_col(s, o, src_row, src_col):
        return pltpu.make_async_remote_copy(
            src_ref=gather.at[src_row, src_col],
            dst_ref=gather.at[src_row, src_col],
            send_sem=f_send.at[s, o - 1],
            recv_sem=g_recv.at[src_row, src_col],
            device_id={"cols": lax.rem(col + o, cols)},
            device_id_type=MESH,
        )

    for i in range(rows - 1):
        o = 1 + (rows // 2 - 1 + i) % (rows - 1)
        spread_row(o, row).start()
    for o in range(1, cols):
        spread_col(0, o, row, col).start()

    ns = (scalars[...].astype(F32) + message(0, s_ch)).astype(BF)
    out_scalars[...] = ns
    energy = jnp.dot(
        read_scalar[...], ns.astype(F32), preferred_element_type=F32, precision=HIGHEST
    ) + jnp.dot(read_vector[...], square, preferred_element_type=F32, precision=HIGHEST)
    pose_iota = lax.broadcasted_iota(jnp.int32, (pose_pad, blk), 0)
    energies[me] = jnp.where(
        jnp.broadcast_to(pose_row, (pose_pad, blk)) == pose_iota,
        jnp.broadcast_to(energy, (pose_pad, blk)),
        0.0,
    )

    def energy_copy(q, src):
        return pltpu.make_async_remote_copy(
            src_ref=energies.at[src],
            dst_ref=energies.at[src],
            send_sem=e_send.at[q],
            recv_sem=e_recv.at[src],
            device_id=peer(q)[1],
            device_id_type=MESH,
        )

    def energy_start(q, carry):
        energy_copy(q, me).start()
        return carry

    def energy_wait(q, carry):
        energy_copy(q, peer(q)[0]).wait_recv()
        return carry

    lax.fori_loop(1, total, energy_start, 0)
    force_acc[...] = jnp.zeros_like(force_acc)
    lax.fori_loop(1, total, energy_wait, 0)
    sums = energies[0]
    for q in range(1, total):
        sums = sums + energies[q]
    scores = jnp.broadcast_to(
        jnp.sum(sums, axis=1, keepdims=True) / POSE_ATOMS, (pose_pad, blk)
    )
    lane_iota = lax.broadcasted_iota(jnp.int32, (pose_pad, blk), 1)
    score_row = jnp.sum(jnp.where(lane_iota == pose_iota, scores, 0.0), axis=0, keepdims=True)
    out_scores[...] = score_row[:, :poses]
    wanted = jnp.zeros((pose_pad, blk), F32)
    for p in range(poses):
        wanted = jnp.where(pose_iota == p, targets[p], wanted)
    resid = scores - wanted

    def gradient(r, c):
        pose = gather[r, c, v3 : v3 + 16].astype(F32)[0:1]
        member = jnp.broadcast_to(pose, (pose_pad, blk)) == pose_iota.astype(F32)
        node_resid = jnp.sum(jnp.where(member, resid, 0.0), axis=0, keepdims=True)
        scale = 2.0 * node_resid * rv_col[...]
        return [
            (scale * gather[r, c, d * v_ch : (d + 1) * v_ch].astype(F32)).astype(BF).astype(F32)
            for d in range(3)
        ]

    own_grad = gradient(row, col)
    for d in range(3):
        force_norm[d : d + 1] = jnp.sum(norm_buf[...] * own_grad[d], axis=0, keepdims=True)

    def backward(r, c):
        grad = gradient(r, c)
        weights = [fwb[s_ch + v_ch :, k * blk : (k + 1) * blk] for k in range(shells)]
        left = jnp.concatenate(
            [
                jnp.concatenate([(grad[d] * w).astype(BF) for w in weights], axis=1)
                for d in range(3)
            ],
            axis=0,
        )
        found = [find(r, c, t) for t in range(windows)]
        table = jnp.concatenate([one_hot(code, 1) for code, _ in found], axis=0)
        back = lax.dot_general(
            left, table, (((1,), (1,)), ((), ())), preferred_element_type=F32
        )
        for t, (_, src) in enumerate(found):
            gp = gate_pos[src]
            for d in range(3):
                piece = back[d * v_ch : (d + 1) * v_ch, t * blk : (t + 1) * blk]
                term = jnp.sum(gp * piece, axis=0, keepdims=True)
                for q in range(reps):
                    force_acc[q, d : d + 1] += jnp.where(src == q, term, 0.0)

    def backward_step(s, carry):
        r = lax.rem(row + s, rows)

        @pl.when(s > 0)
        def _():
            spread_row(1, r).wait_recv()
            for o in range(1, cols):
                spread_col(s, o, r, col).start()

        backward(r, col)
        for o in range(1, cols):
            c = lax.rem(col + o, cols)
            spread_col(s, o, r, c).wait_recv()
            backward(r, c)
        return carry

    lax.fori_loop(0, rows, backward_step, 0)

    def force_copy(o, src):
        return pltpu.make_async_remote_copy(
            src_ref=force_acc.at[lax.rem(rep + o, reps)],
            dst_ref=force_recv.at[src],
            send_sem=q_send.at[o],
            recv_sem=q_recv.at[src],
            device_id={"reps": lax.rem(rep + o, reps)},
            device_id_type=MESH,
        )

    for o in range(1, reps):
        force_copy(o, rep).start()

    for o in range(1, reps):
        for c in panel_copies(lax.rem(rep + o, reps), rep):
            c.wait_send()
    for s in range(rows):
        for o in range(1, cols):
            cross(s, o, False).wait_send()
            spread_col(s, o, lax.rem(row + s, rows), col).wait_send()
        if s < rows - 1:
            along(s, row).wait_send()
            spread_row(s + 1, row).wait_send()

    def energy_sent(q, carry):
        energy_copy(q, me).wait_send()
        return carry

    lax.fori_loop(1, total, energy_sent, 0)

    back = force_acc[rep]
    for o in range(1, reps):
        src = lax.rem(rep + o, reps)
        force_copy(o, src).wait_recv()
        back = back + force_recv[src]
    out_forces[...] = force_norm[0:3] - back[0:3]
    for o in range(1, reps):
        force_copy(o, rep).wait_send()


def local(
    scalars, vectors, positions, node_pose, source_block, target_block, block_count, shell_codes,
    weight_in, message_weight, filter_weights, read_scalar, read_vector, targets,
):
    rows, reps, cols = (lax.axis_size(name) for name in ("rows", "reps", "cols"))
    total = rows * reps * cols
    s_ch, blk = scalars.shape
    v_ch = vectors.shape[1]
    v3 = 3 * v_ch
    out_rows = s_ch + v3 + v_ch
    shells = filter_weights.shape[0]
    slots = shell_codes.shape[0]
    poses = targets.shape[0]
    pose_pad = -(-poses // 8) * 8
    width = shells * blk
    vmem = pl.BlockSpec(memory_space=pltpu.VMEM)
    smem = pl.BlockSpec(memory_space=pltpu.SMEM)
    anywhere = pl.BlockSpec(memory_space=pl.ANY)
    dma = pltpu.SemaphoreType.DMA
    new_scalars, new_vectors, scores, forces = pl.pallas_call(
        functools.partial(kernel, rows, reps, cols, poses, shells),
        out_shape=(
            jax.ShapeDtypeStruct((s_ch, blk), BF),
            jax.ShapeDtypeStruct((v3, blk), BF),
            jax.ShapeDtypeStruct((1, poses), F32),
            jax.ShapeDtypeStruct((3, blk), F32),
        ),
        in_specs=[vmem] * 4 + [smem] * 3 + [anywhere] + [vmem] * 5 + [smem],
        out_specs=(vmem,) * 4,
        scratch_shapes=[
            pltpu.VMEM((slots, blk, blk), jnp.int32),
            pltpu.VMEM((reps, s_ch, blk), BF),
            pltpu.VMEM((reps, v3, blk), BF),
            pltpu.VMEM((reps, 8, blk), F32),
            pltpu.VMEM((reps, v_ch, blk), F32),
            pltpu.VMEM((reps, out_rows, width), BF),
            pltpu.VMEM((s_ch + 2 * v_ch, width), F32),
            pltpu.VMEM((v_ch, blk), F32),
            pltpu.VMEM((rows, cols - 1, out_rows, blk), BF),
            pltpu.VMEM((rows, cols - 1, out_rows, blk), BF),
            pltpu.VMEM((rows, out_rows, blk), F32),
            pltpu.VMEM((rows, out_rows, blk), BF),
            pltpu.VMEM((rows, out_rows, blk), BF),
            pltpu.VMEM((v_ch, blk), F32),
            pltpu.VMEM((rows, cols, v3 + 16, blk), BF),
            pltpu.VMEM((total, pose_pad, blk), F32),
            pltpu.VMEM((reps, 8, blk), F32),
            pltpu.VMEM((reps, 8, blk), F32),
            pltpu.VMEM((8, blk), F32),
            dma,
            dma((3, reps)),
            dma((3, reps)),
            dma((rows, cols - 1)),
            dma((rows, cols - 1)),
            dma((rows,)),
            dma((rows,)),
            dma((rows,)),
            dma((rows, cols)),
            dma((rows, cols - 1)),
            dma((total,)),
            dma((total,)),
            dma((reps,)),
            dma((reps,)),
        ],
        compiler_params=pltpu.CompilerParams(
            collective_id=0, has_side_effects=True, vmem_limit_bytes=56 * 1024 * 1024
        ),
        name="layer",
    )(
        scalars, vectors.reshape(v3, blk), positions, node_pose.reshape(1, blk),
        source_block, target_block, block_count, shell_codes,
        weight_in, message_weight, filter_weights,
        read_scalar.reshape(1, s_ch), read_vector.reshape(1, v_ch), targets,
    )
    return (
        new_scalars, new_vectors.reshape(3, v_ch, blk), scores.reshape(poses), forces,
    )


def solution(mesh):
    spread = ("groups", "rows", "reps", "cols")
    placed = (
        P(None, spread),
        P(None, None, spread),
        P(None, spread),
        P(spread),
        P(spread),
        P(spread),
        P(spread),
        P(spread, None, None),
        P(),
        P(),
        P(),
        P(),
        P(),
        P("groups"),
    )
    return jax.shard_map(
        local,
        mesh=mesh,
        in_specs=placed,
        out_specs=(P(None, spread), P(None, None, spread), P("groups"), P(None, spread)),
        check_vma=False,
    )
```

time: 236 us -> 51.2 us (0.22)
  blocking collectives: 61.1 us -> 0 us
  matrix products: 57.4 us -> 0 us
  Pallas kernels: 0 us -> 46.5 us
  local copies, waits for them, and re-layouts: 49.3 us -> 3.25 us
  waiting for transfers between devices: 32.9 us -> 0 us
  between operations: 15.1 us -> 1.3 us
  other arithmetic: 12.9 us -> 0 us
  starting transfers between devices: 5.73 us -> 0 us
    dot_general x17 -> x0, matrix products: 57.4 us -> none  [the longest x4 22 us: forward_step(): jnp.einsum('ep,ecb->pcb', place_hot, term, precision=lax.Precision.HIGHEST)]
    pallas_call x0 -> x1, Pallas kernels: none -> 46.5 us  [local(): pl.pallas_call(functools.partial(kernel, rows, reps, cols, poses, shells)...]
    psum x1 -> x0, blocking collectives: 31.3 us -> none  [local(): lax.psum(jnp.sum(member * energy[None], axis=1), ('rows', 'reps', 'cols'))]
    all_gather x4 -> x0, blocking collectives: 29.7 us -> none  [the longest x1 14.5 us: local(): lax.all_gather(grad_vec.reshape(1, 3 * vector_width, block_width), ('rows...]
    all_to_all x1 -> x0, waiting for transfers between devices: 25.5 us -> none  [local(): lax.all_to_all(partial_value, ('rows', 'cols'), split_axis=0, concat_axis...]
    gather x8 -> x0, local copies, waits for them, and re-layouts: 15.2 us -> none  [the longest x4 12.8 us: forward_step(): left = jnp.take(panel_rows, source_part, axis=0)]
    mul x13 -> x0, local copies, waits for them, and re-layouts: 14.5 us -> none  [the longest x5 7.69 us: filtered(): gate_pos[..., None, :, None, :] * positions[..., :, None, None, :]]
    reduce_scatter x1 -> x0, waiting for transfers between devices: 7.35 us -> none  [local(): lax.psum_scatter(back_panel.astype(jnp.bfloat16), 'reps', scatter_dimensi...]
  transfers between devices with their start and end apart: 2 -> 0, of which waited for: 2 -> 0; matrix products, arithmetic and copies ran while one was open for 0% -> 0% of each run, Pallas kernels for 0% -> 0%
where the time goes in v1:
time: 51.2 us; the launch traced here: 51 us
  Pallas kernels  46.5 us (91%)
  local copies, waits for them, and re-layouts  3.25 us (6%)
  between operations  1.3 us (3%)
    pallas_call x1, Pallas kernels, local(): pl.pallas_call(functools.partial(kernel, rows, reps, cols, poses, shells)...  46.5 us
    unnamed x10, local copies, waits for them, and re-layouts  3.25 us

profile of v1, /device:TPU:0, one launch (start us, length us, event | category | flops | bytes accessed | tf_op | source)
XLA Modules:
  0.0 51.0 jit_solution(18381651151133343451)
XLA Ops:
  1.3 46.5 %layer.1 = (bf16[256,128]{1,0:T(8,128)(2,1)}, bf16[192,128]{1,0:T(8,128)(2,1)}, f32[1,4]{1,0:T(1,128)}, f32[3,128]{1,0:T(4,128)}) custom-call(bf16[256,128]{1,0:T(8,128)(2,1)} %scalars.1, bf16[192,128]{1,0:T(8,128)(2,1)} %bitcast.6, bf16[3,128]{1,0:T(4,128)(2,1)} %positions.1, s32[1,128]{1,0:T(1,128)} %bitcast.9, s32[16]{0:T(128)} %source_block.1, ...), custom_call_target="tpu_custom_call" | custom-call | tf_op jit(solution)/shard_map/layer/pallas_call | solution.py:422
  47.8 0.0 copy-start
  47.8 1.5 %copy.23 = bf16[256,128]{1,0:T(8,128)(2,1)} copy(bf16[256,128]{1,0:T(8,128)(2,1)} %get-tuple-element.16) | data formatting | bytes 131072
  49.3 0.0 copy-done
  49.3 0.0 copy-start.2
  49.3 0.0 copy-start.1
  49.3 0.6 %copy.24 = bf16[3,64,128]{2,1,0:T(8,128)(2,1)} copy(bf16[3,64,128]{2,1,0:T(8,128)(2,1)S(1)} %bitcast.7) | data formatting | bytes 98304
  49.9 0.0 copy-done.2
  49.9 0.5 %copy.25 = f32[4]{0:T(128)} copy(f32[4]{0:T(128)S(1)} %bitcast.11) | data formatting | bytes 32
  50.4 0.0 copy-done.1
  50.4 0.6 %copy.26 = f32[3,128]{1,0:T(4,128)} copy(f32[3,128]{1,0:T(4,128)S(1)} %copy-done.1) | data formatting | bytes 3072
Async XLA Ops:
  47.8 1.5 %copy-start = (bf16[192,128]{1,0:T(8,128)(2,1)S(1)}, bf16[192,128]{1,0:T(8,128)(2,1)}, u32[]{:S(2)}) copy-start(bf16[192,128]{1,0:T(8,128)(2,1)} %get-tuple-element.9) | copy-start | bytes 147460
  49.3 0.7 %copy-start.2 = (f32[1,4]{1,0:T(1,128)S(1)}, f32[1,4]{1,0:T(1,128)}, u32[]{:S(2)}) copy-start(f32[1,4]{1,0:T(1,128)} %get-tuple-element.10) | copy-start | bytes 52
  49.3 1.2 %copy-start.1 = (f32[3,128]{1,0:T(4,128)S(1)}, f32[3,128]{1,0:T(4,128)}, u32[]{:S(2)}) copy-start(f32[3,128]{1,0:T(4,128)} %get-tuple-element.19) | copy-start | bytes 4612

commit v2 on v1

--- a/solution.py
+++ b/solution.py
@@ -19,7 +19,7 @@
     scalars, vectors, positions, node_pose, source_block, target_block, block_count, codes_hbm,
     weight_in, message_weight, filter_weights, read_scalar, read_vector, targets,
     out_scalars, out_vectors, out_scores, out_forces,
-    codes, panel_s, panel_v, panel_p, gate_pos, rows_f, fwb, rv_col, xsend, xrecv, own, ssend, recv,
+    codes, tables, sources, panel_s, panel_v, panel_p, gate_pos, rows_f, fwb, rv_col, xsend, xrecv, own, ssend, recv,
     norm_buf, gather, energies, force_acc, force_recv, force_norm,
     codes_sem, panel_send, panel_recv, x_send, x_recv, s_send, s_recv,
     g_send, g_recv, f_send, e_send, e_recv, q_send, q_recv,
@@ -36,7 +36,7 @@
     slots = codes.shape[0]
     places = rows * cols
     windows = -(-slots // places)
-    pose_pad = energies.shape[1]
+    pose_pad = -(-poses // 8) * 8
 
     def peer(q):
         flat = lax.rem(me + q, total)
@@ -71,9 +71,10 @@
 
     pl.semaphore_wait(barrier, total - 1)
 
-    def panel_copies(q, src_rep):
+    def panel_copies(q, src_rep, which=(0, 1, 2)):
         out = []
-        for a, buf in enumerate((panel_s, panel_v, panel_p)):
+        for a in which:
+            buf = (panel_s, panel_v, panel_p)[a]
             out.append(
                 pltpu.make_async_remote_copy(
                     src_ref=buf.at[src_rep],
@@ -90,7 +91,10 @@
         for c in panel_copies(lax.rem(rep + o, reps), rep):
             c.start()
 
-    def make_rows(q):
+    def make_rows(q, remote):
+        if remote:
+            panel_copies(q, q, (0,))[0].wait_recv()
+
         hidden = jnp.dot(weight_in[...], panel_s[q], preferred_element_type=F32)
         hidden = (hidden / (1.0 + jnp.exp(-hidden))).astype(BF)
         gates = jnp.dot(message_weight[...], hidden, preferred_element_type=F32).astype(BF)
@@ -99,62 +103,70 @@
         gv = gates[s_ch : s_ch + v_ch]
         gp = gates[s_ch + v_ch :]
         gate_pos[q] = gp
+        if remote:
+            for c in panel_copies(q, q, (1, 2)):
+                c.wait_recv()
+
         pos = panel_p[q]
         vec = panel_v[q].astype(F32)
         gvv = [gv * vec[d * v_ch : (d + 1) * v_ch] for d in range(3)]
         gpp = [gp * pos[d : d + 1] for d in range(3)]
         for k in range(shells):
             span = pl.ds(k * blk, blk)
-            rows_f[q, 0:s_ch, span] = (gs * fwb[0:s_ch, span]).astype(BF)
+            rows_f[q, 1, :, span] = (gs * fwb[0:s_ch, span]).astype(BF)
             wv = fwb[s_ch : s_ch + v_ch, span]
             wp = fwb[s_ch + v_ch :, span]
             for d in range(3):
-                rows_f[q, s_ch + d * v_ch : s_ch + (d + 1) * v_ch, span] = (
+                rows_f[q, 0, d * v_ch : (d + 1) * v_ch, span] = (
                     gvv[d] * wv + gpp[d] * wp
                 ).astype(BF)
-            rows_f[q, s_ch + v3 :, span] = (gp * wp).astype(BF)
-
-    def rows_step(o, carry):
-        q = lax.rem(rep + o, reps)
-
-        @pl.when(o > 0)
-        def _():
-            for c in panel_copies(q, q):
-                c.wait_recv()
-
-        make_rows(q)
-        return carry
-
-    lax.fori_loop(0, reps, rows_step, 0)
-    codes_copy.wait()
-
-    def find(r, c, t):
-        wanted = (r * reps + rep) * cols + c
+            rows_f[q, 0, v3:, span] = (gp * wp).astype(BF)
+
+    def find(dr, o, t):
+        wanted = (lax.rem(row + dr, rows) * reps + rep) * cols + lax.rem(col + o, cols)
         slot = jnp.int32(0)
         found = jnp.int32(0)
-        for o in range(t * places, min((t + 1) * places, slots)):
-            hit = (target_block[o] == wanted) & (o < block_count[0])
-            slot = jnp.where(hit, o, slot)
+        for e in range(t * places, min((t + 1) * places, slots)):
+            hit = (target_block[e] == wanted) & (e < block_count[0])
+            slot = jnp.where(hit, e, slot)
             found = jnp.where(hit, 1, found)
-        src = lax.rem(source_block[slot] // cols, reps)
-        return codes[slot] * found, src
-
-    def one_hot(code, axis):
-        return jnp.concatenate(
-            [jnp.where(code == k + 1, 1.0, 0.0).astype(BF) for k in range(shells)], axis=axis
-        )
-
-    def partial(r, c):
+        return slot, found
+
+    def table_step(dr, carry):
+        for o in range(cols):
+            for t in range(windows):
+                slot, found = find(dr, o, t)
+                sources[dr, o * windows + t] = lax.rem(source_block[slot] // cols, reps)
+                code = codes[slot] * found
+                for k in range(shells):
+                    tables[dr, o * windows + t, k] = jnp.where(code == k + 1, 1.0, 0.0).astype(BF)
+        return carry
+
+    make_rows(rep, None)
+    codes_copy.wait()
+    lax.fori_loop(0, rows, table_step, 0)
+
+    def rows_step(o, carry):
+        make_rows(lax.rem(rep + o, reps), True)
+        return carry
+
+    lax.fori_loop(1, reps, rows_step, 0)
+
+    def partial(h, dr, o):
         acc = None
         for t in range(windows):
-            code, src = find(r, c, t)
-            term = jnp.dot(rows_f[src], one_hot(code, 0), preferred_element_type=F32)
+            src = sources[dr, o * windows + t]
+            table = tables[dr, o * windows + t].reshape(shells * blk, blk)
+            term = jnp.dot(rows_f[src, h], table, preferred_element_type=F32)
             acc = term if acc is None else acc + term
         return acc
 
-    def row_of(s):
-        offset = 1 + lax.rem(rows // 2 - 1 + s, rows - 1)
-        return lax.rem(row + jnp.where(s == rows - 1, 0, offset), rows)
+    def offset_of(u):
+        s = lax.rem(u, rows)
+        return jnp.where(s == rows - 1, 0, 1 + lax.rem(rows // 2 - 1 + s, rows - 1))
+
+    def row_of(u):
+        return lax.rem(row + offset_of(u), rows)
 
     def cross(s, o, arriving):
         if arriving:
@@ -170,51 +182,56 @@
             device_id_type=MESH,
         )
 
-    def along(s, src_row):
+    def along(u, src_row):
+        h = u // rows
         return pltpu.make_async_remote_copy(
-            src_ref=ssend.at[s],
-            dst_ref=recv.at[src_row],
-            send_sem=s_send.at[s],
-            recv_sem=s_recv.at[src_row],
-            device_id={"rows": row_of(s)},
+            src_ref=ssend.at[u],
+            dst_ref=recv.at[h, src_row],
+            send_sem=s_send.at[u],
+            recv_sem=s_recv.at[h, src_row],
+            device_id={"rows": row_of(u)},
             device_id_type=MESH,
         )
 
-    def finish(s):
-        for o in range(1, cols):
-            cross(s, o, True).wait_recv()
-        both = own[s]
-        for o in range(1, cols):
-            both = both + xrecv[s, o - 1].astype(F32)
+    def finish(u):
+        for o in range(1, cols):
+            cross(u, o, True).wait_recv()
+        both = own[u]
+        for o in range(1, cols):
+            both = both + xrecv[u, o - 1].astype(F32)
         return both
 
-    def forward_step(s, carry):
-        r = row_of(s)
-        for o in range(1, cols):
-            xsend[s, o - 1] = partial(r, lax.rem(col + o, cols)).astype(BF)
-            cross(s, o, False).start()
-
-        @pl.when(s > 0)
+    def forward_step(u, carry):
+        h = u // rows
+        dr = offset_of(u)
+        for o in range(1, cols):
+            xsend[u, o - 1] = partial(h, dr, o).astype(BF)
+            cross(u, o, False).start()
+
+        own[u] = partial(h, dr, 0)
+
+        @pl.when(lax.rem(u, rows) < rows - 1)
         def _():
-            ssend[s - 1] = finish(s - 1).astype(BF)
-            along(s - 1, row).start()
-
-        own[s] = partial(r, col)
-        return carry
-
-    lax.fori_loop(0, rows, forward_step, 0)
-    last = rows - 1
-    own[last] = finish(last)
-    for s in range(rows - 1):
-        along(s, row_of(s)).wait_recv()
-
-    def message(lo, hi):
-        acc = own[last, lo:hi]
+            ssend[u] = finish(u).astype(BF)
+            along(u, row).start()
+
+        return carry
+
+    lax.fori_loop(0, 2 * rows, forward_step, 0)
+
+    def arrive(h):
+        own[h * rows + rows - 1] = finish(h * rows + rows - 1)
+        for u in range(h * rows, h * rows + rows - 1):
+            along(u, row_of(u)).wait_recv()
+
+    def message(h, lo, hi):
+        acc = own[h * rows + rows - 1, lo:hi]
         for s in range(rows - 1):
-            acc = acc + recv[row_of(s), lo:hi].astype(F32)
+            acc = acc + recv[h, row_of(s), lo:hi].astype(F32)
         return acc
 
-    norm = message(s_ch + v3, s_ch + v3 + v_ch)
+    arrive(0)
+    norm = message(0, v3, v3 + v_ch)
     norm_buf[...] = norm
     pos_own = panel_p[rep]
     square = jnp.zeros((v_ch, blk), F32)
@@ -222,7 +239,7 @@
         lo = d * v_ch
         nv = (
             vectors[lo : lo + v_ch].astype(F32)
-            + message(s_ch + lo, s_ch + lo + v_ch)
+            + message(0, lo, lo + v_ch)
             - pos_own[d : d + 1] * norm
         ).astype(BF)
         out_vectors[lo : lo + v_ch] = nv
@@ -258,16 +275,27 @@
     for o in range(1, cols):
         spread_col(0, o, row, col).start()
 
-    ns = (scalars[...].astype(F32) + message(0, s_ch)).astype(BF)
+    arrive(1)
+    ns = (scalars[...].astype(F32) + message(1, 0, s_ch)).astype(BF)
     out_scalars[...] = ns
     energy = jnp.dot(
         read_scalar[...], ns.astype(F32), preferred_element_type=F32, precision=HIGHEST
     ) + jnp.dot(read_vector[...], square, preferred_element_type=F32, precision=HIGHEST)
     pose_iota = lax.broadcasted_iota(jnp.int32, (pose_pad, blk), 0)
-    energies[me] = jnp.where(
-        jnp.broadcast_to(pose_row, (pose_pad, blk)) == pose_iota,
-        jnp.broadcast_to(energy, (pose_pad, blk)),
-        0.0,
+    lane_iota = lax.broadcasted_iota(jnp.int32, (pose_pad, blk), 1)
+    by_pose = jnp.sum(
+        jnp.where(
+            jnp.broadcast_to(pose_row, (pose_pad, blk)) == pose_iota,
+            jnp.broadcast_to(energy, (pose_pad, blk)),
+            0.0,
+        ),
+        axis=1,
+        keepdims=True,
+    )
+    energies[me] = jnp.sum(
+        jnp.where(lane_iota == pose_iota, jnp.broadcast_to(by_pose, (pose_pad, blk)), 0.0),
+        axis=0,
+        keepdims=True,
     )
 
     def energy_copy(q, src):
@@ -290,16 +318,27 @@
 
     lax.fori_loop(1, total, energy_start, 0)
     force_acc[...] = jnp.zeros_like(force_acc)
+    for s in range(1, rows):
+        r = lax.rem(row + s, rows)
+        spread_row(1, r).wait_recv()
+        for o in range(1, cols):
+            spread_col(s, o, r, col).start()
     lax.fori_loop(1, total, energy_wait, 0)
     sums = energies[0]
     for q in range(1, total):
         sums = sums + energies[q]
+    score_row = sums / POSE_ATOMS
+    out_scores[...] = score_row[:, :poses]
     scores = jnp.broadcast_to(
-        jnp.sum(sums, axis=1, keepdims=True) / POSE_ATOMS, (pose_pad, blk)
-    )
-    lane_iota = lax.broadcasted_iota(jnp.int32, (pose_pad, blk), 1)
-    score_row = jnp.sum(jnp.where(lane_iota == pose_iota, scores, 0.0), axis=0, keepdims=True)
-    out_scores[...] = score_row[:, :poses]
+        jnp.sum(
+            jnp.where(
+                lane_iota == pose_iota, jnp.broadcast_to(score_row, (pose_pad, blk)), 0.0
+            ),
+            axis=1,
+            keepdims=True,
+        ),
+        (pose_pad, blk),
+    )
     wanted = jnp.zeros((pose_pad, blk), F32)
     for p in range(poses):
         wanted = jnp.where(pose_iota == p, targets[p], wanted)
@@ -319,7 +358,8 @@
     for d in range(3):
         force_norm[d : d + 1] = jnp.sum(norm_buf[...] * own_grad[d], axis=0, keepdims=True)
 
-    def backward(r, c):
+    def backward(s, o):
+        r, c = lax.rem(row + s, rows), lax.rem(col + o, cols)
         grad = gradient(r, c)
         weights = [fwb[s_ch + v_ch :, k * blk : (k + 1) * blk] for k in range(shells)]
         left = jnp.concatenate(
@@ -329,12 +369,18 @@
             ],
             axis=0,
         )
-        found = [find(r, c, t) for t in range(windows)]
-        table = jnp.concatenate([one_hot(code, 1) for code, _ in found], axis=0)
+        table = jnp.concatenate(
+            [
+                jnp.concatenate([tables[s, o * windows + t, k] for k in range(shells)], axis=1)
+                for t in range(windows)
+            ],
+            axis=0,
+        )
         back = lax.dot_general(
             left, table, (((1,), (1,)), ((), ())), preferred_element_type=F32
         )
-        for t, (_, src) in enumerate(found):
+        for t in range(windows):
+            src = sources[s, o * windows + t]
             gp = gate_pos[src]
             for d in range(3):
                 piece = back[d * v_ch : (d + 1) * v_ch, t * blk : (t + 1) * blk]
@@ -345,17 +391,11 @@
     def backward_step(s, carry):
         r = lax.rem(row + s, rows)
 
-        @pl.when(s > 0)
-        def _():
-            spread_row(1, r).wait_recv()
-            for o in range(1, cols):
-                spread_col(s, o, r, col).start()
-
-        backward(r, col)
+        backward(s, 0)
         for o in range(1, cols):
             c = lax.rem(col + o, cols)
             spread_col(s, o, r, c).wait_recv()
-            backward(r, c)
+            backward(s, o)
         return carry
 
     lax.fori_loop(0, rows, backward_step, 0)
@@ -378,11 +418,15 @@
             c.wait_send()
     for s in range(rows):
         for o in range(1, cols):
-            cross(s, o, False).wait_send()
             spread_col(s, o, lax.rem(row + s, rows), col).wait_send()
         if s < rows - 1:
-            along(s, row).wait_send()
             spread_row(s + 1, row).wait_send()
+
+    for u in range(2 * rows):
+        for o in range(1, cols):
+            cross(u, o, False).wait_send()
+        if u % rows < rows - 1:
+            along(u, row).wait_send()
 
     def energy_sent(q, carry):
         energy_copy(q, me).wait_send()
@@ -398,6 +442,12 @@
     out_forces[...] = force_norm[0:3] - back[0:3]
     for o in range(1, reps):
         force_copy(o, rep).wait_send()
+
+
+def publish(*refs):
+    count = len(refs) // 2
+    for source, target in zip(refs[:count], refs[count:]):
+        target[...] = source[...]
 
 
 def local(
@@ -409,17 +459,17 @@
     s_ch, blk = scalars.shape
     v_ch = vectors.shape[1]
     v3 = 3 * v_ch
-    out_rows = s_ch + v3 + v_ch
+    half = s_ch
     shells = filter_weights.shape[0]
     slots = shell_codes.shape[0]
     poses = targets.shape[0]
-    pose_pad = -(-poses // 8) * 8
+    windows = -(-slots // (rows * cols))
     width = shells * blk
     vmem = pl.BlockSpec(memory_space=pltpu.VMEM)
     smem = pl.BlockSpec(memory_space=pltpu.SMEM)
     anywhere = pl.BlockSpec(memory_space=pl.ANY)
     dma = pltpu.SemaphoreType.DMA
-    new_scalars, new_vectors, scores, forces = pl.pallas_call(
+    results = pl.pallas_call(
         functools.partial(kernel, rows, reps, cols, poses, shells),
         out_shape=(
             jax.ShapeDtypeStruct((s_ch, blk), BF),
@@ -431,31 +481,33 @@
         out_specs=(vmem,) * 4,
         scratch_shapes=[
             pltpu.VMEM((slots, blk, blk), jnp.int32),
+            pltpu.VMEM((rows, cols * windows, shells, blk, blk), BF),
+            pltpu.SMEM((rows, cols * windows), jnp.int32),
             pltpu.VMEM((reps, s_ch, blk), BF),
             pltpu.VMEM((reps, v3, blk), BF),
             pltpu.VMEM((reps, 8, blk), F32),
             pltpu.VMEM((reps, v_ch, blk), F32),
-            pltpu.VMEM((reps, out_rows, width), BF),
+            pltpu.VMEM((reps, 2, half, width), BF),
             pltpu.VMEM((s_ch + 2 * v_ch, width), F32),
             pltpu.VMEM((v_ch, blk), F32),
-            pltpu.VMEM((rows, cols - 1, out_rows, blk), BF),
-            pltpu.VMEM((rows, cols - 1, out_rows, blk), BF),
-            pltpu.VMEM((rows, out_rows, blk), F32),
-            pltpu.VMEM((rows, out_rows, blk), BF),
-            pltpu.VMEM((rows, out_rows, blk), BF),
+            pltpu.VMEM((2 * rows, cols - 1, half, blk), BF),
+            pltpu.VMEM((2 * rows, cols - 1, half, blk), BF),
+            pltpu.VMEM((2 * rows, half, blk), F32),
+            pltpu.VMEM((2 * rows, half, blk), BF),
+            pltpu.VMEM((2, rows, half, blk), BF),
             pltpu.VMEM((v_ch, blk), F32),
             pltpu.VMEM((rows, cols, v3 + 16, blk), BF),
-            pltpu.VMEM((total, pose_pad, blk), F32),
+            pltpu.VMEM((total, 1, blk), F32),
             pltpu.VMEM((reps, 8, blk), F32),
             pltpu.VMEM((reps, 8, blk), F32),
             pltpu.VMEM((8, blk), F32),
             dma,
             dma((3, reps)),
             dma((3, reps)),
-            dma((rows, cols - 1)),
-            dma((rows, cols - 1)),
-            dma((rows,)),
-            dma((rows,)),
+            dma((2 * rows, cols - 1)),
+            dma((2 * rows, cols - 1)),
+            dma((2 * rows,)),
+            dma((2, rows)),
             dma((rows,)),
             dma((rows, cols)),
             dma((rows, cols - 1)),
@@ -474,6 +526,13 @@
         weight_in, message_weight, filter_weights,
         read_scalar.reshape(1, s_ch), read_vector.reshape(1, v_ch), targets,
     )
+    new_scalars, new_vectors, scores, forces = pl.pallas_call(
+        publish,
+        out_shape=tuple(jax.ShapeDtypeStruct(x.shape, x.dtype) for x in results),
+        in_specs=[vmem] * 4,
+        out_specs=(vmem,) * 4,
+        name="publish",
+    )(*results)
     return (
         new_scalars, new_vectors.reshape(3, v_ch, blk), scores.reshape(poses), forces,
     )

time: 51.2 us -> 44.5 us (0.87)
  Pallas kernels: 46.5 us -> 43 us
  local copies, waits for them, and re-layouts: 3.25 us -> 0 us
    pallas_call x1, Pallas kernels: 46.5 us -> 41.5 us  [local(): pl.pallas_call(functools.partial(kernel, rows, reps, cols, poses, shells)...]
    unnamed x10 -> x0, local copies, waits for them, and re-layouts: 3.25 us -> none
    pallas_call x0 -> x1, Pallas kernels: none -> 1.53 us  [local(): pl.pallas_call(publish, out_shape=tuple((jax.ShapeDtypeStruct(x.shape, x....]
where the time goes in v2:
time: 44.5 us; the launch traced here: 44.3 us
  Pallas kernels  43 us (97%)
  between operations  1.29 us (3%)
    pallas_call x1, Pallas kernels, local(): pl.pallas_call(functools.partial(kernel, rows, reps, cols, poses, shells)...  41.5 us
    pallas_call x1, Pallas kernels, local(): pl.pallas_call(publish, out_shape=tuple((jax.ShapeDtypeStruct(x.shape, x....  1.53 us

profile of v2, /device:TPU:0, one launch (start us, length us, event | category | flops | bytes accessed | tf_op | source)
XLA Modules:
  0.0 44.3 jit_solution(14580796049575942325)
XLA Ops:
  1.3 41.5 %layer.1 = (bf16[256,128]{1,0:T(8,128)(2,1)}, bf16[192,128]{1,0:T(8,128)(2,1)}, f32[1,4]{1,0:T(1,128)}, f32[3,128]{1,0:T(4,128)}) custom-call(bf16[256,128]{1,0:T(8,128)(2,1)} %scalars.1, bf16[192,128]{1,0:T(8,128)(2,1)} %bitcast.6, bf16[3,128]{1,0:T(4,128)(2,1)} %positions.1, s32[1,128]{1,0:T(1,128)} %bitcast.8, s32[16]{0:T(128)} %source_block.1, ...), custom_call_target="tpu_custom_call" | custom-call | tf_op jit(solution)/shard_map/layer/pallas_call | solution.py:472
  42.8 1.5 %publish.1 = (bf16[256,128]{1,0:T(8,128)(2,1)}, bf16[192,128]{1,0:T(8,128)(2,1)}, f32[1,4]{1,0:T(1,128)}, f32[3,128]{1,0:T(4,128)}) custom-call(bf16[256,128]{1,0:T(8,128)(2,1)} %get-tuple-element.12.refs_0_, bf16[192,128]{1,0:T(8,128)(2,1)} %get-tuple-element.13.refs_1_, f32[1,4]{1,0:T(1,128)} %get-tuple-element.14.refs_2_, f32[3,128]{1,0:T(4,128)} %get-tuple-element.15.refs_3_), custom_call_target="tpu_custom_call" | custom-call | tf_op jit(solution)/shard_map/publish/pallas_call | solution.py:529

commit v3 on v2

--- a/solution.py
+++ b/solution.py
@@ -11,7 +11,6 @@
 BF = jnp.bfloat16
 F32 = jnp.float32
 MESH = pl.DeviceIdType.MESH
-HIGHEST = lax.Precision.HIGHEST
 
 
 def kernel(
@@ -19,7 +18,7 @@
     scalars, vectors, positions, node_pose, source_block, target_block, block_count, codes_hbm,
     weight_in, message_weight, filter_weights, read_scalar, read_vector, targets,
     out_scalars, out_vectors, out_scores, out_forces,
-    codes, tables, sources, panel_s, panel_v, panel_p, gate_pos, rows_f, fwb, rv_col, xsend, xrecv, own, ssend, recv,
+    codes, tables, turned, sources, picked, live, panel_s, panel_v, panel_p, gate_pos, rows_f, fwb, rv_col, rs_col, xsend, xrecv, own, ssend, recv,
     norm_buf, gather, energies, force_acc, force_recv, force_norm,
     codes_sem, panel_send, panel_recv, x_send, x_recv, s_send, s_recv,
     g_send, g_recv, f_send, e_send, e_recv, q_send, q_recv,
@@ -69,6 +68,8 @@
     rv_row = jnp.concatenate([read_vector[...], jnp.zeros((1, 128 - v_ch), F32)], axis=1)
     rv_col[...] = jnp.transpose(jnp.broadcast_to(rv_row, (blk, 128)))[:v_ch]
 
+    rs_col[...] = jnp.transpose(jnp.broadcast_to(read_scalar[...], (blk, s_ch)))
+
     pl.semaphore_wait(barrier, total - 1)
 
     def panel_copies(q, src_rep, which=(0, 1, 2)):
@@ -137,9 +138,22 @@
             for t in range(windows):
                 slot, found = find(dr, o, t)
                 sources[dr, o * windows + t] = lax.rem(source_block[slot] // cols, reps)
+                picked[dr, o * windows + t] = slot
+                live[dr, o * windows + t] = found
                 code = codes[slot] * found
                 for k in range(shells):
                     tables[dr, o * windows + t, k] = jnp.where(code == k + 1, 1.0, 0.0).astype(BF)
+        return carry
+
+    def turn_step(dr, carry):
+        for o in range(cols):
+            for t in range(windows):
+                code = codes[picked[dr, o * windows + t]] * live[dr, o * windows + t]
+                code = jnp.transpose(code.astype(F32))
+                for k in range(shells):
+                    turned[dr, o, k, :, t * blk : (t + 1) * blk] = jnp.where(
+                        code == float(k + 1), 1.0, 0.0
+                    ).astype(BF)
         return carry
 
     make_rows(rep, None)
@@ -201,14 +215,20 @@
             both = both + xrecv[u, o - 1].astype(F32)
         return both
 
+    ahead = min(2, 2 * rows)
+
+    def cross_step(u, carry):
+        for o in range(1, cols):
+            xsend[u, o - 1] = partial(u // rows, offset_of(u), o).astype(BF)
+            cross(u, o, False).start()
+        return carry
+
     def forward_step(u, carry):
-        h = u // rows
-        dr = offset_of(u)
-        for o in range(1, cols):
-            xsend[u, o - 1] = partial(h, dr, o).astype(BF)
-            cross(u, o, False).start()
-
-        own[u] = partial(h, dr, 0)
+        @pl.when(u + ahead < 2 * rows)
+        def _():
+            cross_step(u + ahead, 0)
+
+        own[u] = partial(u // rows, offset_of(u), 0)
 
         @pl.when(lax.rem(u, rows) < rows - 1)
         def _():
@@ -217,7 +237,9 @@
 
         return carry
 
+    lax.fori_loop(0, ahead, cross_step, 0)
     lax.fori_loop(0, 2 * rows, forward_step, 0)
+    lax.fori_loop(0, rows, turn_step, 0)
 
     def arrive(h):
         own[h * rows + rows - 1] = finish(h * rows + rows - 1)
@@ -275,12 +297,11 @@
     for o in range(1, cols):
         spread_col(0, o, row, col).start()
 
+    vector_energy = jnp.sum(rv_col[...] * square, axis=0, keepdims=True)
     arrive(1)
     ns = (scalars[...].astype(F32) + message(1, 0, s_ch)).astype(BF)
     out_scalars[...] = ns
-    energy = jnp.dot(
-        read_scalar[...], ns.astype(F32), preferred_element_type=F32, precision=HIGHEST
-    ) + jnp.dot(read_vector[...], square, preferred_element_type=F32, precision=HIGHEST)
+    energy = vector_energy + jnp.sum(rs_col[...] * ns.astype(F32), axis=0, keepdims=True)
     pose_iota = lax.broadcasted_iota(jnp.int32, (pose_pad, blk), 0)
     lane_iota = lax.broadcasted_iota(jnp.int32, (pose_pad, blk), 1)
     by_pose = jnp.sum(
@@ -323,6 +344,9 @@
         spread_row(1, r).wait_recv()
         for o in range(1, cols):
             spread_col(s, o, r, col).start()
+    for s in range(rows):
+        for o in range(1, cols):
+            spread_col(s, o, lax.rem(row + s, rows), lax.rem(col + o, cols)).wait_recv()
     lax.fori_loop(1, total, energy_wait, 0)
     sums = energies[0]
     for q in range(1, total):
@@ -369,16 +393,8 @@
             ],
             axis=0,
         )
-        table = jnp.concatenate(
-            [
-                jnp.concatenate([tables[s, o * windows + t, k] for k in range(shells)], axis=1)
-                for t in range(windows)
-            ],
-            axis=0,
-        )
-        back = lax.dot_general(
-            left, table, (((1,), (1,)), ((), ())), preferred_element_type=F32
-        )
+        table = turned[s, o].reshape(shells * blk, windows * blk)
+        back = jnp.dot(left, table, preferred_element_type=F32)
         for t in range(windows):
             src = sources[s, o * windows + t]
             gp = gate_pos[src]
@@ -389,16 +405,11 @@
                     force_acc[q, d : d + 1] += jnp.where(src == q, term, 0.0)
 
     def backward_step(s, carry):
-        r = lax.rem(row + s, rows)
-
-        backward(s, 0)
-        for o in range(1, cols):
-            c = lax.rem(col + o, cols)
-            spread_col(s, o, r, c).wait_recv()
+        for o in range(cols):
             backward(s, o)
         return carry
 
-    lax.fori_loop(0, rows, backward_step, 0)
+    lax.fori_loop(0, rows, backward_step, 0, unroll=2 if rows % 2 == 0 else 1)
 
     def force_copy(o, src):
         return pltpu.make_async_remote_copy(
@@ -482,6 +493,9 @@
         scratch_shapes=[
             pltpu.VMEM((slots, blk, blk), jnp.int32),
             pltpu.VMEM((rows, cols * windows, shells, blk, blk), BF),
+            pltpu.VMEM((rows, cols, shells, blk, windows * blk), BF),
+            pltpu.SMEM((rows, cols * windows), jnp.int32),
+            pltpu.SMEM((rows, cols * windows), jnp.int32),
             pltpu.SMEM((rows, cols * windows), jnp.int32),
             pltpu.VMEM((reps, s_ch, blk), BF),
             pltpu.VMEM((reps, v3, blk), BF),
@@ -490,6 +504,7 @@
             pltpu.VMEM((reps, 2, half, width), BF),
             pltpu.VMEM((s_ch + 2 * v_ch, width), F32),
             pltpu.VMEM((v_ch, blk), F32),
+            pltpu.VMEM((s_ch, blk), F32),
             pltpu.VMEM((2 * rows, cols - 1, half, blk), BF),
             pltpu.VMEM((2 * rows, cols - 1, half, blk), BF),
             pltpu.VMEM((2 * rows, half, blk), F32),

time: 44.5 us -> 41.6 us (0.935)
  Pallas kernels: 43 us -> 40.2 us
    pallas_call x1, Pallas kernels: 41.5 us -> 38.6 us  [local(): pl.pallas_call(functools.partial(kernel, rows, reps, cols, poses, shells)...]
where the time goes in v3:
time: 41.6 us; the launch traced here: 41.4 us
  Pallas kernels  40.2 us (97%)
  between operations  1.29 us (3%)
    pallas_call x1, Pallas kernels, local(): pl.pallas_call(functools.partial(kernel, rows, reps, cols, poses, shells)...  38.6 us
    pallas_call x1, Pallas kernels, local(): pl.pallas_call(publish, out_shape=tuple((jax.ShapeDtypeStruct(x.shape, x....  1.53 us

profile of v3, /device:TPU:0, one launch (start us, length us, event | category | flops | bytes accessed | tf_op | source)
XLA Modules:
  0.0 41.4 jit_solution(4655176854791983945)
XLA Ops:
  1.3 38.6 %layer.1 = (bf16[256,128]{1,0:T(8,128)(2,1)}, bf16[192,128]{1,0:T(8,128)(2,1)}, f32[1,4]{1,0:T(1,128)}, f32[3,128]{1,0:T(4,128)}) custom-call(bf16[256,128]{1,0:T(8,128)(2,1)} %scalars.1, bf16[192,128]{1,0:T(8,128)(2,1)} %bitcast.6, bf16[3,128]{1,0:T(4,128)(2,1)} %positions.1, s32[1,128]{1,0:T(1,128)} %bitcast.8, s32[16]{0:T(128)} %source_block.1, ...), custom_call_target="tpu_custom_call" | custom-call | tf_op jit(solution)/shard_map/layer/pallas_call | solution.py:483
  39.9 1.5 %publish.1 = (bf16[256,128]{1,0:T(8,128)(2,1)}, bf16[192,128]{1,0:T(8,128)(2,1)}, f32[1,4]{1,0:T(1,128)}, f32[3,128]{1,0:T(4,128)}) custom-call(bf16[256,128]{1,0:T(8,128)(2,1)} %get-tuple-element.12.refs_0_, bf16[192,128]{1,0:T(8,128)(2,1)} %get-tuple-element.13.refs_1_, f32[1,4]{1,0:T(1,128)} %get-tuple-element.14.refs_2_, f32[3,128]{1,0:T(4,128)} %get-tuple-element.15.refs_3_), custom_call_target="tpu_custom_call" | custom-call | tf_op jit(solution)/shard_map/publish/pallas_call | solution.py:544

commit v4 on v3

--- a/solution.py
+++ b/solution.py
@@ -292,8 +292,7 @@
         )
 
     for i in range(rows - 1):
-        o = 1 + (rows // 2 - 1 + i) % (rows - 1)
-        spread_row(o, row).start()
+        spread_row(i + 1, row).start()
     for o in range(1, cols):
         spread_col(0, o, row, col).start()
 
@@ -409,7 +408,7 @@
             backward(s, o)
         return carry
 
-    lax.fori_loop(0, rows, backward_step, 0, unroll=2 if rows % 2 == 0 else 1)
+    lax.fori_loop(0, rows, backward_step, 0, unroll=4 if rows % 4 == 0 else 1)
 
     def force_copy(o, src):
         return pltpu.make_async_remote_copy(

time: 41.6 us -> 41.4 us (level)
  no operation moved by 1% of the time
where the time goes in v4:
time: 41.4 us; the launch traced here: 41.2 us
  Pallas kernels  39.9 us (96%)
  between operations  1.29 us (3%)
    pallas_call x1, Pallas kernels, local(): pl.pallas_call(functools.partial(kernel, rows, reps, cols, poses, shells)...  38.4 us
    pallas_call x1, Pallas kernels, local(): pl.pallas_call(publish, out_shape=tuple((jax.ShapeDtypeStruct(x.shape, x....  1.53 us

profile of v4, /device:TPU:0, one launch (start us, length us, event | category | flops | bytes accessed | tf_op | source)
XLA Modules:
  0.0 41.2 jit_solution(9924907508823788669)
XLA Ops:
  1.3 38.4 %layer.1 = (bf16[256,128]{1,0:T(8,128)(2,1)}, bf16[192,128]{1,0:T(8,128)(2,1)}, f32[1,4]{1,0:T(1,128)}, f32[3,128]{1,0:T(4,128)}) custom-call(bf16[256,128]{1,0:T(8,128)(2,1)} %scalars.1, bf16[192,128]{1,0:T(8,128)(2,1)} %bitcast.6, bf16[3,128]{1,0:T(4,128)(2,1)} %positions.1, s32[1,128]{1,0:T(1,128)} %bitcast.8, s32[16]{0:T(128)} %source_block.1, ...), custom_call_target="tpu_custom_call" | custom-call | tf_op jit(solution)/shard_map/layer/pallas_call | solution.py:482
  39.6 1.5 %publish.1 = (bf16[256,128]{1,0:T(8,128)(2,1)}, bf16[192,128]{1,0:T(8,128)(2,1)}, f32[1,4]{1,0:T(1,128)}, f32[3,128]{1,0:T(4,128)}) custom-call(bf16[256,128]{1,0:T(8,128)(2,1)} %get-tuple-element.12.refs_0_, bf16[192,128]{1,0:T(8,128)(2,1)} %get-tuple-element.13.refs_1_, f32[1,4]{1,0:T(1,128)} %get-tuple-element.14.refs_2_, f32[3,128]{1,0:T(4,128)} %get-tuple-element.15.refs_3_), custom_call_target="tpu_custom_call" | custom-call | tf_op jit(solution)/shard_map/publish/pallas_call | solution.py:543
